TPU v7x, 256 devices: a whole 4x4x8 slice. The times are simulated.
256 devices in a mesh: dp: 8 (over y, core), expert: 32 (over x, z).
Axes of the slice: x: 4, y: 4, z: 8, core: 2. Of those that a mesh axis runs over, the one named last changes fastest.
Arguments:
- tokens: bfloat16 [32768, 2048], P(('dp', 'expert')), may hold values from -9 to 9
- out_grad: bfloat16 [32768, 2048], P(('dp', 'expert')), may hold values from -1.8 to 1.8
- probs: bfloat16 [32768, 8], P(('dp', 'expert')), may hold values from 0.019897461 to 0.5
- expert_ids: int32 [32768, 8], P(('dp', 'expert')), may hold values from 0 to 31, all different within a row; in each aligned block of 128 rows (0 to 127, 128 to 255, ...) at most 40 rows name the same one
- dropped: int32 [32768, 8], P(('dp', 'expert')), may hold values 0 or 1
- preacts: bfloat16 [8, 32, 1280, 768], P('dp', 'expert'), may hold values from -6 to 6
- w_gu: bfloat16 [32, 2048, 768], P('expert', 'dp'), may hold values from -0.125 to 0.125
- w_down: bfloat16 [32, 384, 2048], P('expert', None, 'dp'), may hold values from -0.3125 to 0.3125
Outputs:
- tok_grad: bfloat16 [32768, 2048], P(('dp', 'expert'))
- prob_grad: bfloat16 [32768, 8], P(('dp', 'expert'))
- grad_gu: float32 [32, 2048, 768], P('expert', 'dp')
- grad_down: float32 [32, 384, 2048], P('expert', None, 'dp')
- mean_square: float32 [], replicated
Inputs may be any that keep to these rules, and one draw needn't show every extreme that they name: `expert_ids`: each row names 8 different experts. Within the rows of one device no expert is named more than 40 times, a bound that some block reaches in every draw.
All inputs are finite; a program needn't handle non-finite values. No bound on the sum of `dropped` on one device may be relied on, other than what follows from the above.
Results may differ from a plain program's by a relative error of at most 0.017.
Values may be sent and summed in bfloat16 or wider, within the bound.
No kernel may reach another device: no remote copies, remote signals or barrier semaphores. Data moves between devices by JAX's collectives and lax.ppermute only.
A program may use at most 128 MiB of HBM per device.

v0:
```python
import jax
import jax.numpy as jnp
from jax import lax
from jax.sharding import PartitionSpec as P

FW = 384
EXPERTS = 32
CAP = 40


def slot_match(expert_ids, dropped, experts, capacity):
    tok_rows, top_k = expert_ids.shape
    flat_ids = expert_ids.reshape(-1)
    onehot = (flat_ids[:, None] == jnp.arange(experts, dtype=jnp.int32)[None, :]).astype(jnp.int32)
    before = jnp.cumsum(onehot, axis=0) - onehot
    position = jnp.sum(before * onehot, axis=1)
    slot_ids = flat_ids * capacity + position
    slot_ids = jnp.where(dropped.reshape(-1) == 0, slot_ids, -1).reshape(tok_rows, top_k)
    every_slot = jnp.arange(experts * capacity, dtype=jnp.int32)
    return (every_slot[:, None, None] == slot_ids[None, :, :]).astype(jnp.float32)


def body(tokens, out_grad, probs, expert_ids, dropped, preacts, w_gu, w_down):
    expert_count = lax.axis_size("expert")
    local_experts = EXPERTS // expert_count
    model_width = tokens.shape[1]
    matches = slot_match(expert_ids, dropped, EXPERTS, CAP)
    counts_bf = jnp.sum(matches, axis=2).astype(jnp.bfloat16)
    x_bins = jnp.dot(counts_bf, tokens, preferred_element_type=jnp.float32).astype(jnp.bfloat16)
    grad_bins = jnp.dot(counts_bf, out_grad, preferred_element_type=jnp.float32).astype(
        jnp.bfloat16
    )
    prob_bins = jnp.einsum("qtk,tk->q", matches, probs.astype(jnp.float32)).astype(jnp.bfloat16)
    x_in, grad_in, prob_in = (
        lax.all_to_all(
            x_bins.reshape(EXPERTS, CAP, model_width),
            "expert",
            split_axis=0,
            concat_axis=0,
            tiled=True,
        ),
        lax.all_to_all(
            grad_bins.reshape(EXPERTS, CAP, model_width),
            "expert",
            split_axis=0,
            concat_axis=0,
            tiled=True,
        ),
        lax.all_to_all(
            prob_bins.reshape(EXPERTS, CAP), "expert", split_axis=0, concat_axis=0, tiled=True
        ),
    )
    x_in = x_in.reshape(expert_count, local_experts, CAP, model_width)
    grad_in = grad_in.reshape(expert_count, local_experts, CAP, model_width)
    prob_in = prob_in.reshape(expert_count, local_experts, CAP)
    w_gu_full, w_down_full = (
        lax.all_gather(w_gu, "dp", axis=1, tiled=True),
        lax.all_gather(w_down, "dp", axis=2, tiled=True),
    )
    pre_acts = preacts.reshape(local_experts, expert_count, CAP, 2 * FW)
    proj = jnp.einsum("jecd,efd->ejcf", grad_in, w_down_full, preferred_element_type=jnp.float32)
    gate_pre = pre_acts[..., :FW].astype(jnp.float32)
    up_pre = pre_acts[..., FW:].astype(jnp.float32)
    sigmoid_a = jax.nn.sigmoid(gate_pre)
    silu_a = gate_pre * sigmoid_a
    hidden = silu_a * up_pre
    slot_prob = jnp.sum(hidden * proj, axis=-1).astype(jnp.bfloat16)
    weight_p = jnp.transpose(prob_in, (1, 0, 2)).astype(jnp.float32)[..., None]
    scaled = weight_p * proj
    dgu = jnp.concatenate(
        [scaled * up_pre * sigmoid_a * (1.0 + gate_pre * (1.0 - sigmoid_a)), scaled * silu_a],
        axis=-1,
    ).astype(jnp.bfloat16)
    hidden_p = (weight_p * hidden).astype(jnp.bfloat16)
    grad_down_term = jnp.einsum(
        "ejcf,jecd->efd", hidden_p, grad_in, preferred_element_type=jnp.float32
    )
    grad_gu_term = jnp.einsum("jecd,ejcf->edf", x_in, dgu, preferred_element_type=jnp.float32)
    grad_gu = lax.psum_scatter(
        grad_gu_term.astype(jnp.bfloat16), "dp", scatter_dimension=1, tiled=True
    ).astype(jnp.float32)
    grad_down = lax.psum_scatter(
        grad_down_term.astype(jnp.bfloat16), "dp", scatter_dimension=2, tiled=True
    ).astype(jnp.float32)
    grad_gu, grad_down = (grad_gu, grad_down)
    slot_grad = jnp.einsum(
        "ejcf,edf->jecd", dgu, w_gu_full, preferred_element_type=jnp.float32
    ).astype(jnp.bfloat16)
    prob_slot = jnp.transpose(slot_prob, (1, 0, 2))
    grad_back = lax.all_to_all(slot_grad, "expert", split_axis=0, concat_axis=1, tiled=True)
    prob_back = lax.all_to_all(prob_slot, "expert", split_axis=0, concat_axis=1, tiled=True)
    grad_flat = grad_back.reshape(EXPERTS * CAP, model_width)
    tok_grad = jnp.einsum(
        "qt,qd->td", counts_bf, grad_flat, preferred_element_type=jnp.float32
    ).astype(jnp.bfloat16)
    prob_grad = jnp.einsum("qtk,q->tk", matches, prob_back.reshape(-1).astype(jnp.float32)).astype(
        jnp.bfloat16
    )
    tok_grad, prob_grad = (tok_grad, prob_grad)
    partial_sq = jnp.sum(grad_gu * grad_gu) + jnp.sum(grad_down * grad_down)
    total = lax.psum(partial_sq, ("dp", "expert"))
    mean_square = total / (EXPERTS * 3 * model_width * FW)
    return (tok_grad, prob_grad, grad_gu, grad_down, mean_square)


def solution(mesh):
    return jax.shard_map(
        body,
        mesh=mesh,
        in_specs=(
            P(("dp", "expert"), None),
            P(("dp", "expert"), None),
            P(("dp", "expert"), None),
            P(("dp", "expert"), None),
            P(("dp", "expert"), None),
            P("dp", "expert", None, None),
            P("expert", "dp", None),
            P("expert", None, "dp"),
        ),
        out_specs=(
            P(("dp", "expert"), None),
            P(("dp", "expert"), None),
            P("expert", "dp", None),
            P("expert", None, "dp"),
            P(),
        ),
        check_vma=False,
    )
```

profile of v0, /device:TPU:1, one launch (start us, length us, event | category | flops | bytes accessed | tf_op | source)
XLA Modules:
  0.0 512.5 jit_solution(15231709304935841768)
XLA Ops:
  7.2 0.0 copy-start
  7.2 0.0 copy-start.3
  7.2 0.8 copy.54
  8.0 0.1 eq.53
  8.1 0.1 eq.49
  8.2 9.0 %reduce-window.6 = s32[32,8,128]{2,1,0:T(8,128)S(1)} reduce-window(s32[32,8,128]{2,1,0:T(8,128)S(1)} %fusion.28, s32[]{:T(128)} %constant.6.clone.1), window={size=1x1x128 pad=0_0x0_0x127_0}, to_apply=%region_0.0 | reduce-window | flops 4161536 | bytes 262148 | tf_op jit(solution)/shard_map/reduce-window
  17.3 0.1 slice.16
  17.4 0.1 copy.56
  17.5 0.1 copy.57
  17.6 0.1 broadcast_add_fusion
  17.8 0.1 reduce_sum.48
  17.9 0.7 add_select_fusion
  18.6 0.9 iota_compare_fusion
  19.5 0.0 copy-done.3
  19.5 0.8 fusion.16
  20.3 0.7 all_to_all.32
  21.0 11.9 %all-to-all-start = ((bf16[32,1,40]{2,1,0:T(2,128)(2,1)}), bf16[32,1,40]{2,1,0:T(2,128)(2,1)S(1)}, u32[]{:S(2)}, u32[]{:S(2)}) async-start(bf16[32,1,40]{2,1,0:T(2,128)(2,1)} %all_to_all.32), calls=%async_computation | async-start | bytes 32768 | tf_op jit(solution)/shard_map/all_to_all | solution.py:49
  32.9 6.7 %convert_reduce_fusion = bf16[1280,128]{1,0:T(8,128)(2,1)S(1)} fusion(s32[128,8]{0,1:T(8,128)S(1)} %add_select_fusion), kind=kLoop, calls=%fused_computation.5 | loop fusion | flops 3768320 | bytes 331776 | tf_op jit(solution)/shard_map/reduce_sum | solution.py:28
  39.6 0.0 copy-done
  39.6 3.9 convolution_convert_fusion.1
  43.5 0.0 all-to-all-done
  43.5 0.0 copy-start.1
  43.5 9.5 %all-to-all-start.1 = ((bf16[32,40,2048]{2,1,0:T(8,128)(2,1)}), bf16[32,40,2048]{2,1,0:T(8,128)(2,1)}, u32[]{:S(2)}, u32[]{:S(2)}) async-start(bf16[32,40,2048]{2,1,0:T(8,128)(2,1)} %bitcast.87), calls=%async_computation.1 | async-start | bytes 10485760 | tf_op jit(solution)/shard_map/all_to_all | solution.py:42
  53.0 0.0 copy-done.1
  53.0 3.8 convolution_convert_fusion
  56.8 111.1 %all-to-all-done.1 = bf16[32,40,2048]{2,1,0:T(8,128)(2,1)} async-done(((bf16[32,40,2048]{2,1,0:T(8,128)(2,1)}), bf16[32,40,2048]{2,1,0:T(8,128)(2,1)}, u32[]{:S(2)}, u32[]{:S(2)}) %all-to-all-start.1) | async-done | bytes 5242912 | tf_op jit(solution)/shard_map/all_to_all | solution.py:42
  167.9 0.0 copy-start.2
  168.0 10.3 %all-to-all-start.4 = ((bf16[32,40,2048]{2,1,0:T(8,128)(2,1)}), bf16[32,40,2048]{2,1,0:T(8,128)(2,1)}, u32[]{:S(2)}, u32[]{:S(2)}) async-start(bf16[32,40,2048]{2,1,0:T(8,128)(2,1)} %bitcast.86), calls=%async_computation.4 | async-start | bytes 10485760 | tf_op jit(solution)/shard_map/all_to_all | solution.py:35
  178.3 0.0 all-gather.3.cloned.1.call-start
  178.3 0.7 all-gather.3.cloned.1.call-update
  179.0 0.2 all-gather.5.cloned.1.call-start
  179.2 0.5 all-gather.5.cloned.1.call-update
  179.8 31.4 %all-gather.3.cloned.1.call-done = bf16[1,384,2048]{2,1,0:T(8,128)(2,1)} async-done(((bf16[1,384,256]{2,1,0:T(8,128)(2,1)}), bf16[1,384,2048]{2,1,0:T(8,128)(2,1)}) %all-gather.3.cloned.1.call-update) | async-done | bytes 1572880 | tf_op jit(solution)/shard_map/all_gather | solution.py:58
  211.2 0.0 copy-done.2
  211.2 8.2 %fusion.23 = (bf16[32,40,384]{2,1,0:T(8,128)(2,1)}, bf16[32,40,384]{2,1,0:T(8,128)(2,1)}, bf16[32,40]{1,0:T(8,128)(2,1)S(1)}) fusion(f32[32,40]{1,0:T(8,128)S(1)} %bitcast.90, bf16[1,32,40,768]{3,2,1,0:T(8,128)(2,1)S(1)} %bitcast.93, bf16[32,40,2048]{2,1,0:T(8,128)(2,1)} %all-to-all-done.1, bf16[1,384,2048]{2,1,0:T(8,128)(2,1)} %all-gather.3.cloned.1.call-done), kind=kOutput, calls=%fused_computation.38 | convolution fusion | flops 2022603520 | bytes 10755584 | tf_op jit(solution)/shard_map/jecd,efd->ejcf/dot_general | solution.py:61
  219.4 0.6 copy.61
  220.0 73.6 %all-to-all-done.4 = bf16[32,40,2048]{2,1,0:T(8,128)(2,1)} async-done(((bf16[32,40,2048]{2,1,0:T(8,128)(2,1)}), bf16[32,40,2048]{2,1,0:T(8,128)(2,1)}, u32[]{:S(2)}, u32[]{:S(2)}) %all-to-all-start.4) | async-done | bytes 5242912 | tf_op jit(solution)/shard_map/all_to_all | solution.py:35
  293.6 9.6 %all-to-all-start.3 = ((bf16[32,1,40]{2,1,0:T(2,128)(2,1)}), bf16[32,1,40]{2,1,0:T(2,128)(2,1)S(1)}, u32[]{:S(2)}, u32[]{:S(2)}) async-start(bf16[32,1,40]{2,1,0:T(2,128)(2,1)} %copy.61), calls=%async_computation.3 | async-start | bytes 32768 | tf_op jit(solution)/shard_map/all_to_all | solution.py:91
  303.3 0.0 all-gather.5.cloned.1.call-done
  303.3 9.1 %convert_bitcast_fusion = bf16[32,1,40,2048]{3,2,1,0:T(8,128)(2,1)} fusion(bf16[1,2048,768]{2,1,0:T(8,128)(2,1)} %all-gather.5.cloned.1.call-done, bf16[32,40,384]{2,1,0:T(8,128)(2,1)} %get-tuple-element.10, bf16[32,40,384]{2,1,0:T(8,128)(2,1)} %get-tuple-element.9), kind=kOutput, calls=%fused_computation.4 | convolution fusion | flops 4033085440 | bytes 10354688 | tf_op jit(solution)/shard_map/ejcf,edf->jecd/dot_general | solution.py:86
  312.4 0.0 all-to-all-done.3
  312.4 9.3 %all-to-all-start.2 = ((bf16[32,1,40,2048]{3,2,1,0:T(8,128)(2,1)}), bf16[32,1,40,2048]{3,2,1,0:T(8,128)(2,1)}, u32[]{:S(2)}, u32[]{:S(2)}) async-start(bf16[32,1,40,2048]{3,2,1,0:T(8,128)(2,1)} %convert_bitcast_fusion), calls=%async_computation.2 | async-start | bytes 10485760 | tf_op jit(solution)/shard_map/all_to_all | solution.py:90
  321.8 0.0 reduce-scatter.5.cloned.1.call-start
  321.8 6.2 %fusion.4 = bf16[1,384,2048]{2,1,0:T(8,128)(2,1)} fusion(bf16[32,40,2048]{2,1,0:T(8,128)(2,1)} %all-to-all-done.1, f32[32,40]{1,0:T(8,128)S(1)} %bitcast.91, bf16[1,32,40,768]{3,2,1,0:T(8,128)(2,1)S(1)} %bitcast.94), kind=kOutput, calls=%fused_computation.15 | convolution fusion | flops 2018476032 | bytes 8786944 | tf_op jit(solution)/shard_map/ejcf,jecd->efd/dot_general | solution.py:75
  328.0 0.0 reduce-scatter.5.cloned.1.call-update
  328.0 0.3 reduce-scatter.3.cloned.1.call-start
  328.3 9.1 %fusion.3 = bf16[1,2048,768]{2,1,0:T(8,128)(2,1)} fusion(bf16[32,40,2048]{2,1,0:T(8,128)(2,1)} %all-to-all-done.4, bf16[32,40,384]{2,1,0:T(8,128)(2,1)} %get-tuple-element.10, bf16[32,40,384]{2,1,0:T(8,128)(2,1)} %get-tuple-element.9), kind=kOutput, calls=%fused_computation.11 | convolution fusion | flops 4032036864 | bytes 10354688 | tf_op jit(solution)/shard_map/jecd,ejcf->edf/dot_general | solution.py:78
  337.4 0.0 reduce-scatter.3.cloned.1.call-update
  337.4 0.1 reduce.3
  337.4 0.1 reshape.136
  337.6 27.1 %reduce-scatter.5.cloned.1.call-done = bf16[1,384,256]{2,1,0:T(8,128)(2,1)} async-done(((bf16[1,384,2048]{2,1,0:T(8,128)(2,1)}), bf16[1,384,256]{2,1,0:T(8,128)(2,1)}) %reduce-scatter.5.cloned.1.call-update) | async-done | bytes 196624 | tf_op jit(solution)/shard_map/reduce_scatter | solution.py:82
  364.7 2.3 multiply_reduce_fusion.1
  367.0 38.2 %reduce-scatter.3.cloned.1.call-done = bf16[1,256,768]{2,1,0:T(8,128)(2,1)} async-done(((bf16[1,2048,768]{2,1,0:T(8,128)(2,1)}), bf16[1,256,768]{2,1,0:T(8,128)(2,1)}) %reduce-scatter.3.cloned.1.call-update) | async-done | bytes 393232 | tf_op jit(solution)/shard_map/reduce_scatter | solution.py:79
  405.2 2.6 multiply_reduce_fusion
  409.1 4.2 select_reduce_fusion
  413.3 86.7 %psum.7 = f32[]{:T(128)} all-reduce(f32[]{:T(128)S(6)} %add.23), channel_id=1, replica_groups=mesh['dp'=8,'expert'=32] {'dp','expert'}, use_global_device_ids=true, to_apply=%region_9.10 | all-reduce | flops 1 | bytes 8 | tf_op jit(solution)/shard_map/psum | solution.py:101
  500.7 0.0 all-to-all-done.2
  500.7 4.2 convolution_convert_fusion.2
  (7 shorter events, 0.2 us)
Async XLA Ops:
  7.2 32.4 %copy-start = (bf16[128,2048]{1,0:T(8,128)(2,1)S(1)}, bf16[128,2048]{1,0:T(8,128)(2,1)}, u32[]{:S(2)}) copy-start(bf16[128,2048]{1,0:T(8,128)(2,1)} %param.9) | copy-start | bytes 1572868
  7.2 12.3 %copy-start.3 = (bf16[128,8]{0,1:T(8,128)(2,1)S(1)}, bf16[128,8]{0,1:T(8,128)(2,1)}, u32[]{:S(2)}) copy-start(bf16[128,8]{0,1:T(8,128)(2,1)} %param.10) | copy-start | bytes 6148
  21.0 22.5 %all-to-all-start = ((bf16[32,1,40]{2,1,0:T(2,128)(2,1)}), bf16[32,1,40]{2,1,0:T(2,128)(2,1)S(1)}, u32[]{:S(2)}, u32[]{:S(2)}) async-start(bf16[32,1,40]{2,1,0:T(2,128)(2,1)} %all_to_all.32), calls=%async_computation | async-start | bytes 32768 | tf_op jit(solution)/shard_map/all_to_all | solution.py:49
  43.5 9.5 %copy-start.1 = (bf16[128,2048]{1,0:T(8,128)(2,1)S(1)}, bf16[128,2048]{1,0:T(8,128)(2,1)}, u32[]{:S(2)}) copy-start(bf16[128,2048]{1,0:T(8,128)(2,1)} %param.8) | copy-start | bytes 1572868
  43.5 124.4 %all-to-all-start.1 = ((bf16[32,40,2048]{2,1,0:T(8,128)(2,1)}), bf16[32,40,2048]{2,1,0:T(8,128)(2,1)}, u32[]{:S(2)}, u32[]{:S(2)}) async-start(bf16[32,40,2048]{2,1,0:T(8,128)(2,1)} %bitcast.87), calls=%async_computation.1 | async-start | bytes 10485760 | tf_op jit(solution)/shard_map/all_to_all | solution.py:42
  167.9 43.3 %copy-start.2 = (bf16[1,1,1280,768]{3,2,1,0:T(8,128)(2,1)S(1)}, bf16[1,1,1280,768]{3,2,1,0:T(8,128)(2,1)}, u32[]{:S(2)}) copy-start(bf16[1,1,1280,768]{3,2,1,0:T(8,128)(2,1)} %param.13) | copy-start | bytes 5898244
  168.0 125.7 %all-to-all-start.4 = ((bf16[32,40,2048]{2,1,0:T(8,128)(2,1)}), bf16[32,40,2048]{2,1,0:T(8,128)(2,1)}, u32[]{:S(2)}, u32[]{:S(2)}) async-start(bf16[32,40,2048]{2,1,0:T(8,128)(2,1)} %bitcast.86), calls=%async_computation.4 | async-start | bytes 10485760 | tf_op jit(solution)/shard_map/all_to_all | solution.py:35
  178.3 32.9 %all-gather.3.cloned.1.call-start = ((), (), s32[]{:S(2)}) async-start(), calls=%async_computation.7 | async-start | bytes 1769472 | tf_op jit(solution)/shard_map/all_gather | solution.py:58
  179.0 124.3 %all-gather.5.cloned.1.call-start = ((), (), s32[]{:S(2)}) async-start(), calls=%async_computation.8 | async-start | bytes 3538944 | tf_op jit(solution)/shard_map/all_gather | solution.py:57
  293.6 18.8 %all-to-all-start.3 = ((bf16[32,1,40]{2,1,0:T(2,128)(2,1)}), bf16[32,1,40]{2,1,0:T(2,128)(2,1)S(1)}, u32[]{:S(2)}, u32[]{:S(2)}) async-start(bf16[32,1,40]{2,1,0:T(2,128)(2,1)} %copy.61), calls=%async_computation.3 | async-start | bytes 32768 | tf_op jit(solution)/shard_map/all_to_all | solution.py:91
  312.4 188.2 %all-to-all-start.2 = ((bf16[32,1,40,2048]{3,2,1,0:T(8,128)(2,1)}), bf16[32,1,40,2048]{3,2,1,0:T(8,128)(2,1)}, u32[]{:S(2)}, u32[]{:S(2)}) async-start(bf16[32,1,40,2048]{3,2,1,0:T(8,128)(2,1)} %convert_bitcast_fusion), calls=%async_computation.2 | async-start | bytes 10485760 | tf_op jit(solution)/shard_map/all_to_all | solution.py:90
  321.8 42.9 %reduce-scatter.5.cloned.1.call-start = ((), (), s32[]{:S(2)}) async-start(), calls=%async_computation.10 | async-start | bytes 1769472 | tf_op jit(solution)/shard_map/reduce_scatter | solution.py:82
  328.0 77.2 %reduce-scatter.3.cloned.1.call-start = ((), (), s32[]{:S(2)}) async-start(), calls=%async_computation.9 | async-start | bytes 3538944 | tf_op jit(solution)/shard_map/reduce_scatter | solution.py:79
Sparse Core Ops, SparseCore 0:
  180.9 30.2 all-gather.2
  213.0 31.3 all-gather.4
  328.2 36.4 reduce-scatter.4
  367.1 38.0 reduce-scatter.2
where the time goes:
time: 513 us; the launch traced here: 512 us
  waiting for transfers between devices  283 us (55%)
  blocking collectives  86.7 us (17%)
  starting transfers between devices  51.2 us (10%)
  matrix products  45.2 us (9%)
  other arithmetic  26.7 us (5%)
  between operations  17 us (3%)
    all_to_all x1, waiting for transfers between devices, body(): lax.all_to_all(grad_bins.reshape(EXPERTS, CAP, model_width), 'expert', sp...  111 us
    psum x1, blocking collectives, body(): total = lax.psum(partial_sq, ('dp', 'expert'))  86.7 us
    all_to_all x1, waiting for transfers between devices, body(): lax.all_to_all(x_bins.reshape(EXPERTS, CAP, model_width), 'expert', split...  73.6 us
    reduce_scatter x1, waiting for transfers between devices, body(): lax.psum_scatter(grad_gu_term.astype(jnp.bfloat16), 'dp', scatter_dimensi...  38.2 us
    all_gather x1, waiting for transfers between devices, body(): lax.all_gather(w_down, 'dp', axis=2, tiled=True)  31.4 us
    reduce_scatter x1, waiting for transfers between devices, body(): lax.psum_scatter(grad_down_term.astype(jnp.bfloat16), 'dp', scatter_dimen...  27.1 us
    all_to_all x1, starting transfers between devices, body(): lax.all_to_all(prob_bins.reshape(EXPERTS, CAP), 'expert', split_axis=0, c...  11.9 us
    all_to_all x1, starting transfers between devices, body(): lax.all_to_all(x_bins.reshape(EXPERTS, CAP, model_width), 'expert', split...  10.3 us
  transfers between devices with their start and end apart: 9, of which 5 were waited for; matrix products, arithmetic and copies ran while one was open for 11% of the time, Pallas kernels for 0%

commit v1 on v0

v1 whole, which is shorter than its diff:
```python
import jax
import jax.numpy as jnp
from jax import lax
from jax.sharding import Mesh, PartitionSpec as P

D = 2048
FW = 384
EXPERTS = 32
CAP = 40
TOK = 128
NX = 4
NZ = 8
CHUNKS = 2
WIDTH = D // CHUNKS
BF = jnp.bfloat16
F32 = jnp.float32


def shift(a, step):
    return lax.ppermute(a, "z", [(i, (i + step) % NZ) for i in range(NZ)])


def gather_z(block):
    half = block.shape[1] // 2
    forth, back = block, block
    blocks = [block] + [None] * 7
    for step in (1, 2, 3):
        forth, back = shift(forth, 1), shift(back, -1)
        blocks[NZ - step], blocks[step] = forth, back
    blocks[4] = jnp.concatenate([shift(forth[:, :half], 1), shift(back[:, half:], -1)], axis=1)
    return jnp.stack(blocks)


def add_to(part, got):
    return (part.astype(F32) + got.astype(F32)).astype(BF)


def reduce_z(parts):
    half = parts.shape[2] // 2
    forth, back = shift(parts[4][:, :half], 1), shift(parts[4][:, half:], -1)
    forth = jnp.concatenate([add_to(parts[3][:, :half], forth), parts[3][:, half:]], axis=1)
    back = jnp.concatenate([parts[5][:, :half], add_to(parts[5][:, half:], back)], axis=1)
    for ahead, behind in ((2, 6), (1, 7)):
        forth = add_to(parts[ahead], shift(forth, 1))
        back = add_to(parts[behind], shift(back, -1))
    forth, back = shift(forth, 1), shift(back, -1)
    return (parts[0].astype(F32) + forth.astype(F32) + back.astype(F32)).astype(BF)


def exchange_x(a):
    return lax.all_to_all(a, "x", split_axis=0, concat_axis=0, tiled=True)


def turned(a, axis, start):
    return lax.dynamic_slice_in_dim(jnp.concatenate([a, a], axis=axis), start, NZ, axis)


def slot_map(ids, dropped, probs):
    experts = jnp.arange(EXPERTS, dtype=jnp.int32)
    named = ids.T[None, :, :] == experts[:, None, None]
    routed = jnp.any(named, axis=1)
    kept = jnp.any(named & (dropped.T == 0)[None], axis=1)
    order = jnp.arange(TOK, dtype=jnp.int32)
    earlier = (order[:, None] < order[None, :]).astype(BF)
    position = jnp.dot(routed.astype(BF), earlier, preferred_element_type=F32)
    slots = jnp.where(kept, position, -1.0)
    weights = jnp.sum(jnp.where(named, probs.T.astype(F32)[None], 0.0), axis=1)
    return slots.astype(BF), weights.astype(BF)


def body(tokens, out_grad, probs, expert_ids, dropped, preacts, w_gu, w_down):
    x, z = lax.axis_index("x"), lax.axis_index("z")
    slots, weights = slot_map(expert_ids, dropped, probs)
    info = lax.all_gather(jnp.stack([slots, weights]), ("x", "z"), axis=0, tiled=False)
    w_down_full = lax.all_gather(w_down, ("y", "c"), axis=2, tiled=True)[0]
    w_gu_full = lax.all_gather(w_gu, ("y", "c"), axis=1, tiled=True)[0]
    places = jnp.arange(CAP, dtype=jnp.int32).astype(F32)

    info = info.reshape(NX, NZ, 2, NX, NZ, TOK)
    mine = turned(lax.dynamic_index_in_dim(info[:, :, 0], x, 0, keepdims=False), 0, z)
    mine = lax.dynamic_index_in_dim(mine, z, 2, keepdims=False).astype(F32)
    onehot = (mine[:, :, None, :] == places[None, None, :, None]).astype(BF)
    onehot = onehot.reshape(NZ, NX * CAP, TOK)

    own = lax.dynamic_index_in_dim(lax.dynamic_index_in_dim(info, x, 3, keepdims=False), z, 3, keepdims=False)
    own = turned(own, 1, z).astype(F32)
    held = own[:, :, 0, None, :] == places[None, None, :, None]
    prob_in = jnp.sum(jnp.where(held, own[:, :, 1, None, :], 0.0), axis=-1).reshape(-1)

    pre = turned(preacts.reshape(NX, NZ, CAP, 2 * FW), 1, z).reshape(NX * NZ * CAP, 2 * FW)

    def to_slots(piece):
        blocks = gather_z(piece)
        rows = jnp.einsum("ost,otd->osd", onehot, blocks, preferred_element_type=F32).astype(BF)
        rows = rows.reshape(NZ, NX, CAP, WIDTH).transpose(1, 0, 2, 3)
        return exchange_x(rows.reshape(NX, NZ * CAP, WIDTH)).reshape(NX * NZ * CAP, WIDTH)

    cuts = [slice(i * WIDTH, (i + 1) * WIDTH) for i in range(CHUNKS)]
    grad_in = [to_slots(out_grad[:, cut]) for cut in cuts]
    x_in = [to_slots(tokens[:, cut]) for cut in cuts]

    proj = 0.0
    for cut, piece in zip(cuts, grad_in):
        proj = proj + jnp.einsum("qd,fd->qf", piece, w_down_full[:, cut], preferred_element_type=F32)
    gate_pre = pre[:, :FW].astype(F32)
    up_pre = pre[:, FW:].astype(F32)
    sigmoid_a = jax.nn.sigmoid(gate_pre)
    silu_a = gate_pre * sigmoid_a
    hidden = silu_a * up_pre
    slot_prob = jnp.sum(hidden * proj, axis=-1).astype(BF)
    scaled = prob_in[:, None] * proj
    dgu = jnp.concatenate(
        [scaled * up_pre * sigmoid_a * (1.0 + gate_pre * (1.0 - sigmoid_a)), scaled * silu_a], axis=-1
    ).astype(BF)
    hidden_p = (prob_in[:, None] * hidden).astype(BF)

    tok_grad = []
    for cut in cuts:
        slot_grad = jnp.einsum("qf,df->qd", dgu, w_gu_full[cut], preferred_element_type=F32).astype(BF)
        back = exchange_x(slot_grad.reshape(NX, NZ * CAP, WIDTH))
        back = back.reshape(NX, NZ, CAP, WIDTH).transpose(1, 0, 2, 3).reshape(NZ, NX * CAP, WIDTH)
        parts = jnp.einsum("ost,osd->otd", onehot, back, preferred_element_type=F32).astype(BF)
        tok_grad.append(reduce_z(parts))
    tok_grad = jnp.concatenate(tok_grad, axis=1)

    grad_down = jnp.concatenate(
        [jnp.einsum("qf,qd->fd", hidden_p, p, preferred_element_type=F32) for p in grad_in], axis=1
    ).astype(BF)
    grad_gu = jnp.concatenate(
        [jnp.einsum("qd,qf->df", p, dgu, preferred_element_type=F32) for p in x_in], axis=0
    ).astype(BF)
    grad_down = lax.psum_scatter(grad_down[None], ("y", "c"), scatter_dimension=2, tiled=True).astype(F32)
    grad_gu = lax.psum_scatter(grad_gu[None], ("y", "c"), scatter_dimension=1, tiled=True).astype(F32)

    straight = turned(slot_prob.reshape(NX, NZ, CAP), 1, (NZ - z) % NZ)
    prob_all = lax.all_gather(straight, ("x", "z"), axis=0, tiled=False)
    prob_all = lax.dynamic_index_in_dim(prob_all, x, 1, keepdims=False)
    prob_all = lax.dynamic_index_in_dim(prob_all, z, 1, keepdims=False).astype(F32)
    hit = slots.astype(F32)[:, None, :] == places[None, :, None]
    by_expert = jnp.sum(jnp.where(hit, prob_all[:, :, None], 0.0), axis=1)
    experts = jnp.arange(EXPERTS, dtype=jnp.int32)
    named = expert_ids.T[:, None, :] == experts[None, :, None]
    prob_grad = jnp.sum(jnp.where(named, by_expert[None], 0.0), axis=1).T.astype(BF)

    partial_sq = jnp.sum(grad_gu * grad_gu) + jnp.sum(grad_down * grad_down)
    total = lax.psum(partial_sq, ("y", "c", "x", "z"))
    mean_square = total / (EXPERTS * 3 * D * FW)
    return tok_grad, prob_grad, grad_gu, grad_down, mean_square


def solution(mesh):
    split = Mesh(mesh.devices.reshape(4, 2, NX, NZ), ("y", "c", "x", "z"))
    rows = P(("y", "c", "x", "z"), None)
    gu, down = P(("x", "z"), ("y", "c"), None), P(("x", "z"), None, ("y", "c"))
    return jax.shard_map(
        body,
        mesh=split,
        in_specs=(rows, rows, rows, rows, rows, P(("y", "c"), ("x", "z"), None, None), gu, down),
        out_specs=(rows, rows, gu, down, P()),
        check_vma=False,
    )
```

time: 513 us -> 502 us (0.979); the launches traced: 512 us -> 492 us
  waiting for transfers between devices: 283 us -> 73.5 us
  blocking collectives: 86.7 us -> 201 us
  local copies, waits for them, and re-layouts: 2.9 us -> 48.2 us
  starting transfers between devices: 51.2 us -> 85.2 us
  other arithmetic: 26.7 us -> 19.3 us
    all_to_all x5 -> x6, waiting for transfers between devices: 185 us -> 35.6 us  [exchange_x(): return lax.all_to_all(a, 'x', split_axis=0, concat_axis=0, tiled=True)]
    all_gather x0 -> x2, blocking collectives: none -> 97.5 us  [the longest x1 53.3 us: body(): prob_all = lax.all_gather(straight, ('x', 'z'), axis=0, tiled=False)]
    reduce_scatter x2, waiting for transfers between devices: 65.4 us -> 0.02 us  [the longest x1 0.02 us: body(): lax.psum_scatter(grad_gu[None], ('y', 'c'), scatter_dimension=1, tiled=True)]
    ppermute x0 -> x48, starting transfers between devices: none -> 58.8 us  [shift(): return lax.ppermute(a, 'z', [(i, (i + step) % NZ) for i in range(NZ)])]
    ppermute x0 -> x48, waiting for transfers between devices: none -> 37.2 us  [shift(): return lax.ppermute(a, 'z', [(i, (i + step) % NZ) for i in range(NZ)])]
    all_gather x2, waiting for transfers between devices: 31.4 us -> 0.02 us  [the longest x1 0.02 us: body(): w_down_full = lax.all_gather(w_down, ('y', 'c'), axis=2, tiled=True)[0]]
    unnamed x9 -> x72, local copies, waits for them, and re-layouts: 0.87 us -> 28.7 us
    all_to_all x5 -> x6, starting transfers between devices: 50.6 us -> 25.9 us  [exchange_x(): return lax.all_to_all(a, 'x', split_axis=0, concat_axis=0, tiled=True)]
  transfers between devices with their start and end apart: 9 -> 58, of which waited for: 5 -> 17; matrix products, arithmetic and copies ran while one was open for 11% -> 22% of each run, Pallas kernels for 0% -> 0%
where the time goes in v1:
time: 502 us; the launch traced here: 492 us
  blocking collectives  201 us (40%)
  starting transfers between devices  85.2 us (17%)
  waiting for transfers between devices  73.5 us (15%)
  local copies, waits for them, and re-layouts  48.2 us (10%)
  matrix products  46.2 us (9%)
  other arithmetic  19.3 us (4%)
  between operations  18.4 us (4%)
    psum x1, blocking collectives, body(): total = lax.psum(partial_sq, ('y', 'c', 'x', 'z'))  103 us
    ppermute x48, starting transfers between devices, shift(): return lax.ppermute(a, 'z', [(i, (i + step) % NZ) for i in range(NZ)])  58.8 us
    all_gather x1, blocking collectives, body(): prob_all = lax.all_gather(straight, ('x', 'z'), axis=0, tiled=False)  53.3 us
    all_gather x1, blocking collectives, body(): lax.all_gather(jnp.stack([slots, weights]), ('x', 'z'), axis=0, tiled=False)  44.2 us
    ppermute x48, waiting for transfers between devices, shift(): return lax.ppermute(a, 'z', [(i, (i + step) % NZ) for i in range(NZ)])  37.2 us
    all_to_all x6, waiting for transfers between devices, exchange_x(): return lax.all_to_all(a, 'x', split_axis=0, concat_axis=0, tiled=True)  35.6 us
    unnamed x72, local copies, waits for them, and re-layouts  28.7 us
    all_to_all x6, starting transfers between devices, exchange_x(): return lax.all_to_all(a, 'x', split_axis=0, concat_axis=0, tiled=True)  25.9 us
  transfers between devices with their start and end apart: 58, of which 17 were waited for; matrix products, arithmetic and copies ran while one was open for 22% of the time, Pallas kernels for 0%

profile of v1, /device:TPU:1, one launch (start us, length us, event | category | flops | bytes accessed | tf_op | source)
XLA Modules:
  0.0 491.6 jit_solution(977050304223873656)
XLA Ops:
  8.0 1.9 fusion.41
  9.8 6.4 %collective-permute-start = (bf16[128,1024]{1,0:T(8,128)(2,1)}, bf16[128,1024]{1,0:T(8,128)(2,1)}, u32[]{:S(2)}, u32[]{:S(2)}) collective-permute-start(bf16[128,1024]{1,0:T(8,128)(2,1)} %get-tuple-element.31), channel_id=1, source_target_pairs={{0,7},{1,0},{2,1},{3,2},{4,3},{5,4},{6,5},{7,6},{8,15},{9,8},{10,9... | collective-permute-start | bytes 786440 | tf_op jit(solution)/shard_map/ppermute | solution.py:20
  16.3 2.7 collective-permute-start.8
  18.9 1.8 fusion.40
  20.8 2.7 collective-permute-start.32
  23.8 44.2 %all-gather = bf16[64,32,128]{2,1,0:T(8,128)(2,1)S(1)} all-gather(bf16[2,32,128]{2,1,0:T(8,128)(2,1)S(1)} %pad_maximum_fusion.8), channel_id=2, replica_groups=mesh['y'=4,'c'=2,'x'=4,'z'=8] {'x','z'}, dimensions={0}, use_global_device_ids=true | all-gather | bytes 540672 | tf_op jit(solution)/shard_map/all_gather | solution.py:74
  76.5 2.2 collective-permute-start.2
  80.4 1.7 bitcast_dynamic-update-slice_fusion.25
  82.0 3.3 collective-permute-done.5
  85.5 2.7 collective-permute-start.7
  89.1 2.7 collective-permute-start.40
  95.2 1.7 bitcast_dynamic-update-slice_fusion.22
  98.6 2.4 convolution_convert_fusion.5
  101.0 1.8 copy.70
  102.8 4.5 all-to-all-start
  109.1 2.7 collective-permute-start.10
  114.1 8.0 %collective-permute-done.13 = bf16[128,1024]{1,0:T(8,128)(2,1)S(1)} collective-permute-done((bf16[128,1024]{1,0:T(8,128)(2,1)}, bf16[128,1024]{1,0:T(8,128)(2,1)S(1)}, u32[]{:S(2)}, u32[]{:S(2)}) %collective-permute-start.13) | collective-permute-done | bytes 262176 | tf_op jit(solution)/shard_map/ppermute | solution.py:20
  122.2 2.7 collective-permute-start.15
  130.1 1.7 bitcast_dynamic-update-slice_fusion.15
  132.5 2.4 convolution_convert_fusion.4
  134.9 1.7 copy.71
  136.7 4.9 %all-to-all-start.1 = ((bf16[4,320,1024]{2,1,0:T(8,128)(2,1)}), bf16[4,320,1024]{2,1,0:T(8,128)(2,1)}, u32[]{:S(2)}, u32[]{:S(2)}) async-start(bf16[4,320,1024]{2,1,0:T(8,128)(2,1)} %bitcast.35), calls=%async_computation.1 | async-start | bytes 5242880 | tf_op jit(solution)/shard_map/all_to_all | solution.py:51
  141.7 2.6 collective-permute-start.34
  144.3 2.7 collective-permute-start.42
  146.9 1.7 bitcast_dynamic-update-slice_fusion.11
  149.6 2.9 collective-permute-done.37
  152.6 2.7 collective-permute-start.39
  155.3 2.8 collective-permute-done.45
  158.2 2.7 collective-permute-start.47
  165.5 2.4 convolution_convert_fusion.3
  168.0 1.7 copy.76
  169.7 5.5 %all-to-all-start.4 = ((bf16[4,320,1024]{2,1,0:T(8,128)(2,1)}), bf16[4,320,1024]{2,1,0:T(8,128)(2,1)}, u32[]{:S(2)}, u32[]{:S(2)}) async-start(bf16[4,320,1024]{2,1,0:T(8,128)(2,1)} %bitcast.78), calls=%async_computation.4 | async-start | bytes 5242880 | tf_op jit(solution)/shard_map/all_to_all | solution.py:51
  178.1 1.8 copy.77
  180.3 4.0 fusion.11
  184.3 11.0 %all-to-all-done.4 = bf16[4,320,1024]{2,1,0:T(8,128)(2,1)} async-done(((bf16[4,320,1024]{2,1,0:T(8,128)(2,1)}), bf16[4,320,1024]{2,1,0:T(8,128)(2,1)}, u32[]{:S(2)}, u32[]{:S(2)}) %all-to-all-start.4) | async-done | bytes 2621472 | tf_op jit(solution)/shard_map/all_to_all | solution.py:51
  195.3 3.7 all-to-all-start.5
  199.2 3.8 fusion.10
  204.4 3.3 fusion.14
  207.7 5.3 %multiply_reduce_fusion = (bf16[1280]{0:T(1024)(128)(2,1)S(1)}, bf16[1280,384]{0,1:T(8,128)(2,1)}, bf16[1280,384]{0,1:T(8,128)(2,1)}) fusion(bf16[1280,384]{0,1:T(8,128)(2,1)S(1)} %copy-done.10, bf16[1280,384]{0,1:T(8,128)(2,1)S(1)} %copy-done.12, f32[1280]{0:T(1024)S(1)} %mul.46, f32[1280,384]{0,1:T(8,128)S(1)} %fusion.14, ...), kind=kOutput, calls=%fused_computation.25 | convolution fusion | flops 1016462080 | bytes 9316864 | tf_op jit(solution)/shard_map/qd,fd->qf/dot_general | solution.py:104
  213.0 5.7 %convolution_convert_fusion.1 = bf16[1280,1024]{1,0:T(8,128)(2,1)} fusion(bf16[1,2048,768]{2,1,0:T(8,128)(2,1)} %all-gather.7.cloned.1.call-done, bf16[1280,384]{0,1:T(8,128)(2,1)} %get-tuple-element.13, bf16[1280,384]{0,1:T(8,128)(2,1)} %get-tuple-element.12), kind=kOutput, calls=%fused_computation.3 | convolution fusion | flops 2018508800 | bytes 6160384 | tf_op jit(solution)/shard_map/qf,df->qd/dot_general | solution.py:119
  218.7 7.5 %all-to-all-done.5 = bf16[4,320,1024]{2,1,0:T(8,128)(2,1)S(1)} async-done(((bf16[4,320,1024]{2,1,0:T(8,128)(2,1)}), bf16[4,320,1024]{2,1,0:T(8,128)(2,1)S(1)}, u32[]{:S(2)}, u32[]{:S(2)}) %all-to-all-start.5) | async-done | bytes 2621472 | tf_op jit(solution)/shard_map/all_to_all | solution.py:51
  227.7 3.7 all-to-all-start.2
  231.4 5.9 %fusion.8 = bf16[1,1024,768]{2,1,0:T(8,128)(2,1)} fusion(bf16[1280,1024]{1,0:T(8,128)(2,1)} %bitcast.79, bf16[1280,384]{0,1:T(8,128)(2,1)} %get-tuple-element.13, bf16[1280,384]{0,1:T(8,128)(2,1)} %get-tuple-element.12), kind=kOutput, calls=%fused_computation.34 | convolution fusion | flops 2017984512 | bytes 6160384 | tf_op jit(solution)/shard_map/qd,qf->df/dot_general | solution.py:130
  237.3 3.8 convolution_convert_fusion
  241.1 17.1 %all-to-all-done.2 = bf16[4,320,1024]{2,1,0:T(8,128)(2,1)S(1)} async-done(((bf16[4,320,1024]{2,1,0:T(8,128)(2,1)}), bf16[4,320,1024]{2,1,0:T(8,128)(2,1)S(1)}, u32[]{:S(2)}, u32[]{:S(2)}) %all-to-all-start.2) | async-done | bytes 2621472 | tf_op jit(solution)/shard_map/all_to_all | solution.py:51
  259.7 3.7 all-to-all-start.3
  263.6 4.7 fusion.9
  268.3 1.8 pad_maximum_fusion
  270.3 53.3 %all-gather.1 = bf16[128,8,40]{2,1,0:T(8,128)(2,1)S(1)} all-gather(bf16[4,8,40]{2,1,0:T(8,128)(2,1)S(1)} %fusion.38), channel_id=3, replica_groups=mesh['y'=4,'c'=2,'x'=4,'z'=8] {'x','z'}, dimensions={0}, use_global_device_ids=true | all-gather | bytes 84480 | tf_op jit(solution)/shard_map/all_gather | solution.py:136
  323.7 2.0 copy.74
  327.4 2.7 collective-permute-start.20
  331.9 2.8 collective-permute-start.28
  335.9 2.6 collective-permute-start.21
  340.1 2.7 collective-permute-start.29
  342.9 3.4 collective-permute-done.17
  346.7 2.4 collective-permute-done.25
  349.6 3.6 collective-permute-done.18
  353.5 2.5 collective-permute-done.26
  359.1 2.7 collective-permute-start.23
  361.8 2.1 collective-permute-done.30
  365.1 2.4 multiply_reduce_fusion.2
  369.4 4.3 collective-permute-done.31
  374.9 2.6 multiply_reduce_fusion.1
  379.7 103.2 %psum.7 = f32[]{:T(128)} all-reduce(f32[]{:T(128)S(6)} %add.132), channel_id=1, replica_groups=mesh['y'=4,'c'=2,'x'=4,'z'=8] {'y','c','x','z'}, use_global_device_ids=true, to_apply=%region_11.12 | all-reduce | flops 1 | bytes 8 | tf_op jit(solution)/shard_map/psum | solution.py:146
  (226 shorter events, 56.7 us)
Async XLA Ops:
  7.2 16.3 %copy-start.18 = (s32[128,8]{0,1:T(8,128)S(1)}, s32[128,8]{0,1:T(8,128)}, u32[]{:S(2)}) copy-start(s32[128,8]{0,1:T(8,128)} %param.12) | copy-start | bytes 12292
  7.2 16.3 %copy-start.19 = (bf16[128,8]{0,1:T(8,128)(2,1)S(1)}, bf16[128,8]{0,1:T(8,128)(2,1)}, u32[]{:S(2)}) copy-start(bf16[128,8]{0,1:T(8,128)(2,1)} %param.10) | copy-start | bytes 6148
  7.2 16.3 %copy-start.17 = (s32[128,8]{0,1:T(8,128)S(1)}, s32[128,8]{0,1:T(8,128)}, u32[]{:S(2)}) copy-start(s32[128,8]{0,1:T(8,128)} %param.11) | copy-start | bytes 12292
  7.2 61.0 %copy-start.7 = (bf16[1,1,1280,768]{3,2,1,0:T(8,128)(2,1)S(1)}, bf16[1,1,1280,768]{3,2,1,0:T(8,128)(2,1)}, u32[]{:S(2)}) copy-start(bf16[1,1,1280,768]{3,2,1,0:T(8,128)(2,1)} %param.13) | copy-start | bytes 5898244
  7.2 197.1 %all-gather.5.cloned.1.call-start = ((), (), s32[]{:S(2)}) async-start(), calls=%async_computation.8 | async-start | bytes 1769472 | tf_op jit(solution)/shard_map/all_gather | solution.py:75
  7.9 205.1 %all-gather.7.cloned.1.call-start = ((), (), s32[]{:S(2)}) async-start(), calls=%async_computation.9 | async-start | bytes 3538944 | tf_op jit(solution)/shard_map/all_gather | solution.py:76
  9.8 60.9 %collective-permute-start = (bf16[128,1024]{1,0:T(8,128)(2,1)}, bf16[128,1024]{1,0:T(8,128)(2,1)}, u32[]{:S(2)}, u32[]{:S(2)}) collective-permute-start(bf16[128,1024]{1,0:T(8,128)(2,1)} %get-tuple-element.31), channel_id=1, source_target_pairs={{0,7},{1,0},{2,1},{3,2},{4,3},{5,4},{6,5},{7,6},{8,15},{9,8},{10,9... | collective-permute-start | bytes 786440 | tf_op jit(solution)/shard_map/ppermute | solution.py:20
  16.2 55.5 %collective-permute-start.3 = (bf16[128,1024]{1,0:T(8,128)(2,1)}, bf16[128,1024]{1,0:T(8,128)(2,1)}, u32[]{:S(2)}, u32[]{:S(2)}) collective-permute-start(bf16[128,1024]{1,0:T(8,128)(2,1)} %get-tuple-element.31), channel_id=1, source_target_pairs={{0,1},{1,2},{2,3},{3,4},{4,5},{5,6},{6,7},{7,0},{8,9},{9,10},{10,1... | collective-permute-start | bytes 786440 | tf_op jit(solution)/shard_map/ppermute | solution.py:20
  16.3 72.7 %collective-permute-start.8 = (bf16[128,1024]{1,0:T(8,128)(2,1)}, bf16[128,1024]{1,0:T(8,128)(2,1)}, u32[]{:S(2)}, u32[]{:S(2)}) collective-permute-start(bf16[128,1024]{1,0:T(8,128)(2,1)} %get-tuple-element.30), channel_id=1, source_target_pairs={{0,7},{1,0},{2,1},{3,2},{4,3},{5,4},{6,5},{7,6},{8,15},{9,8},{10,9... | collective-permute-start | bytes 786440 | tf_op jit(solution)/shard_map/ppermute | solution.py:20
  18.9 70.2 %collective-permute-start.11 = (bf16[128,1024]{1,0:T(8,128)(2,1)}, bf16[128,1024]{1,0:T(8,128)(2,1)S(1)}, u32[]{:S(2)}, u32[]{:S(2)}) collective-permute-start(bf16[128,1024]{1,0:T(8,128)(2,1)} %get-tuple-element.30), channel_id=1, source_target_pairs={{0,1},{1,2},{2,3},{3,4},{4,5},{5,6},{6,7},{7,0},{8,9},{9,10},{10,1... | collective-permute-start | bytes 786440 | tf_op jit(solution)/shard_map/ppermute | solution.py:20
  20.8 88.3 %collective-permute-start.32 = (bf16[128,1024]{1,0:T(8,128)(2,1)}, bf16[128,1024]{1,0:T(8,128)(2,1)S(1)}, u32[]{:S(2)}, u32[]{:S(2)}) collective-permute-start(bf16[128,1024]{1,0:T(8,128)(2,1)} %get-tuple-element.26), channel_id=1, source_target_pairs={{0,7},{1,0},{2,1},{3,2},{4,3},{5,4},{6,5},{7,6},{8,15},{9,8},{10,9... | collective-permute-start | bytes 786440 | tf_op jit(solution)/shard_map/ppermute | solution.py:20
  70.8 5.7 %collective-permute-start.1 = (bf16[128,1024]{1,0:T(8,128)(2,1)}, bf16[128,1024]{1,0:T(8,128)(2,1)}, u32[]{:S(2)}, u32[]{:S(2)}) collective-permute-start(bf16[128,1024]{1,0:T(8,128)(2,1)} %collective-permute-done), channel_id=1, source_target_pairs={{0,7},{1,0},{2,1},{3,2},{4,3},{5,4},{6,5},{7,6},{8,15},{9,8},{10,9... | collective-permute-start | bytes 786440 | tf_op jit(solution)/shard_map/ppermute | solution.py:20
  71.8 6.9 %collective-permute-start.4 = (bf16[128,1024]{1,0:T(8,128)(2,1)}, bf16[128,1024]{1,0:T(8,128)(2,1)}, u32[]{:S(2)}, u32[]{:S(2)}) collective-permute-start(bf16[128,1024]{1,0:T(8,128)(2,1)} %collective-permute-done.3), channel_id=1, source_target_pairs={{0,1},{1,2},{2,3},{3,4},{4,5},{5,6},{6,7},{7,0},{8,9},{9,10},{10,1... | collective-permute-start | bytes 786440 | tf_op jit(solution)/shard_map/ppermute | solution.py:20
  76.5 9.0 %collective-permute-start.2 = (bf16[128,1024]{1,0:T(8,128)(2,1)}, bf16[128,1024]{1,0:T(8,128)(2,1)S(1)}, u32[]{:S(2)}, u32[]{:S(2)}) collective-permute-start(bf16[128,1024]{1,0:T(8,128)(2,1)} %collective-permute-done.1), channel_id=1, source_target_pairs={{0,7},{1,0},{2,1},{3,2},{4,3},{5,4},{6,5},{7,6},{8,15},{9,8},{10,9... | collective-permute-start | bytes 786440 | tf_op jit(solution)/shard_map/ppermute | solution.py:20
  78.7 6.6 %collective-permute-start.5 = (bf16[128,1024]{1,0:T(8,128)(2,1)}, bf16[128,1024]{1,0:T(8,128)(2,1)S(1)}, u32[]{:S(2)}, u32[]{:S(2)}) collective-permute-start(bf16[128,1024]{1,0:T(8,128)(2,1)} %collective-permute-done.4), channel_id=1, source_target_pairs={{0,1},{1,2},{2,3},{3,4},{4,5},{5,6},{6,7},{7,0},{8,9},{9,10},{10,1... | collective-permute-start | bytes 786440 | tf_op jit(solution)/shard_map/ppermute | solution.py:20
  85.3 6.9 %collective-permute-start.6 = (bf16[128,512]{1,0:T(8,128)(2,1)S(1)}, bf16[128,512]{1,0:T(8,128)(2,1)S(1)}, u32[]{:S(2)}, u32[]{:S(2)}) collective-permute-start(bf16[128,512]{1,0:T(8,128)(2,1)S(1)} %slice.213), channel_id=1, source_target_pairs={{0,1},{1,2},{2,3},{3,4},{4,5},{5,6},{6,7},{7,0},{8,9},{9,10},{10,1... | collective-permute-start | bytes 393224 | tf_op jit(solution)/shard_map/ppermute | solution.py:20
  85.5 6.8 %collective-permute-start.7 = (bf16[128,512]{1,0:T(8,128)(2,1)S(1)}, bf16[128,512]{1,0:T(8,128)(2,1)S(1)}, u32[]{:S(2)}, u32[]{:S(2)}) collective-permute-start(bf16[128,512]{1,0:T(8,128)(2,1)S(1)} %slice.214), channel_id=1, source_target_pairs={{0,7},{1,0},{2,1},{3,2},{4,3},{5,4},{6,5},{7,6},{8,15},{9,8},{10,9... | collective-permute-start | bytes 393224 | tf_op jit(solution)/shard_map/ppermute | solution.py:20
  88.9 36.8 %collective-permute-start.35 = (bf16[128,1024]{1,0:T(8,128)(2,1)}, bf16[128,1024]{1,0:T(8,128)(2,1)S(1)}, u32[]{:S(2)}, u32[]{:S(2)}) collective-permute-start(bf16[128,1024]{1,0:T(8,128)(2,1)} %get-tuple-element.26), channel_id=1, source_target_pairs={{0,1},{1,2},{2,3},{3,4},{4,5},{5,6},{6,7},{7,0},{8,9},{9,10},{10,1... | collective-permute-start | bytes 786440 | tf_op jit(solution)/shard_map/ppermute | solution.py:20
  89.1 36.6 %collective-permute-start.40 = (bf16[128,1024]{1,0:T(8,128)(2,1)}, bf16[128,1024]{1,0:T(8,128)(2,1)S(1)}, u32[]{:S(2)}, u32[]{:S(2)}) collective-permute-start(bf16[128,1024]{1,0:T(8,128)(2,1)} %get-tuple-element.27), channel_id=1, source_target_pairs={{0,7},{1,0},{2,1},{3,2},{4,3},{5,4},{6,5},{7,6},{8,15},{9,8},{10,9... | collective-permute-start | bytes 786440 | tf_op jit(solution)/shard_map/ppermute | solution.py:20
  92.3 16.8 %collective-permute-start.9 = (bf16[128,1024]{1,0:T(8,128)(2,1)}, bf16[128,1024]{1,0:T(8,128)(2,1)}, u32[]{:S(2)}, u32[]{:S(2)}) collective-permute-start(bf16[128,1024]{1,0:T(8,128)(2,1)} %collective-permute-done.8), channel_id=1, source_target_pairs={{0,7},{1,0},{2,1},{3,2},{4,3},{5,4},{6,5},{7,6},{8,15},{9,8},{10,9... | collective-permute-start | bytes 786440 | tf_op jit(solution)/shard_map/ppermute | solution.py:20
  92.3 19.5 %collective-permute-start.12 = (bf16[128,1024]{1,0:T(8,128)(2,1)S(1)}, bf16[128,1024]{1,0:T(8,128)(2,1)}, u32[]{:S(2)}, u32[]{:S(2)}) collective-permute-start(bf16[128,1024]{1,0:T(8,128)(2,1)S(1)} %collective-permute-done.11), channel_id=1, source_target_pairs={{0,1},{1,2},{2,3},{3,4},{4,5},{5,6},{6,7},{7,0},{8,9},{9,10},{10,1... | collective-permute-start | bytes 786440 | tf_op jit(solution)/shard_map/ppermute | solution.py:20
  102.8 33.8 %all-to-all-start = ((bf16[4,320,1024]{2,1,0:T(8,128)(2,1)}), bf16[4,320,1024]{2,1,0:T(8,128)(2,1)}, u32[]{:S(2)}, u32[]{:S(2)}) async-start(bf16[4,320,1024]{2,1,0:T(8,128)(2,1)} %bitcast.22), calls=%async_computation | async-start | bytes 5242880 | tf_op jit(solution)/shard_map/all_to_all | solution.py:51
  109.0 18.1 %collective-permute-start.43 = (bf16[128,1024]{1,0:T(8,128)(2,1)}, bf16[128,1024]{1,0:T(8,128)(2,1)}, u32[]{:S(2)}, u32[]{:S(2)}) collective-permute-start(bf16[128,1024]{1,0:T(8,128)(2,1)} %get-tuple-element.27), channel_id=1, source_target_pairs={{0,1},{1,2},{2,3},{3,4},{4,5},{5,6},{6,7},{7,0},{8,9},{9,10},{10,1... | collective-permute-start | bytes 786440 | tf_op jit(solution)/shard_map/ppermute | solution.py:20
  109.1 13.1 %collective-permute-start.10 = (bf16[128,1024]{1,0:T(8,128)(2,1)}, bf16[128,1024]{1,0:T(8,128)(2,1)S(1)}, u32[]{:S(2)}, u32[]{:S(2)}) collective-permute-start(bf16[128,1024]{1,0:T(8,128)(2,1)} %collective-permute-done.9), channel_id=1, source_target_pairs={{0,7},{1,0},{2,1},{3,2},{4,3},{5,4},{6,5},{7,6},{8,15},{9,8},{10,9... | collective-permute-start | bytes 786440 | tf_op jit(solution)/shard_map/ppermute | solution.py:20
  111.7 10.4 %collective-permute-start.13 = (bf16[128,1024]{1,0:T(8,128)(2,1)}, bf16[128,1024]{1,0:T(8,128)(2,1)S(1)}, u32[]{:S(2)}, u32[]{:S(2)}) collective-permute-start(bf16[128,1024]{1,0:T(8,128)(2,1)} %collective-permute-done.12), channel_id=1, source_target_pairs={{0,1},{1,2},{2,3},{3,4},{4,5},{5,6},{6,7},{7,0},{8,9},{9,10},{10,1... | collective-permute-start | bytes 786440 | tf_op jit(solution)/shard_map/ppermute | solution.py:20
  122.1 6.4 %collective-permute-start.14 = (bf16[128,512]{1,0:T(8,128)(2,1)S(1)}, bf16[128,512]{1,0:T(8,128)(2,1)S(1)}, u32[]{:S(2)}, u32[]{:S(2)}) collective-permute-start(bf16[128,512]{1,0:T(8,128)(2,1)S(1)} %slice.216), channel_id=1, source_target_pairs={{0,1},{1,2},{2,3},{3,4},{4,5},{5,6},{6,7},{7,0},{8,9},{9,10},{10,1... | collective-permute-start | bytes 393224 | tf_op jit(solution)/shard_map/ppermute | solution.py:20
  122.2 6.4 %collective-permute-start.15 = (bf16[128,512]{1,0:T(8,128)(2,1)S(1)}, bf16[128,512]{1,0:T(8,128)(2,1)S(1)}, u32[]{:S(2)}, u32[]{:S(2)}) collective-permute-start(bf16[128,512]{1,0:T(8,128)(2,1)S(1)} %slice.217), channel_id=1, source_target_pairs={{0,7},{1,0},{2,1},{3,2},{4,3},{5,4},{6,5},{7,6},{8,15},{9,8},{10,9... | collective-permute-start | bytes 393224 | tf_op jit(solution)/shard_map/ppermute | solution.py:20
  125.7 16.0 %collective-permute-start.33 = (bf16[128,1024]{1,0:T(8,128)(2,1)S(1)}, bf16[128,1024]{1,0:T(8,128)(2,1)}, u32[]{:S(2)}, u32[]{:S(2)}) collective-permute-start(bf16[128,1024]{1,0:T(8,128)(2,1)S(1)} %collective-permute-done.32), channel_id=1, source_target_pairs={{0,7},{1,0},{2,1},{3,2},{4,3},{5,4},{6,5},{7,6},{8,15},{9,8},{10,9... | collective-permute-start | bytes 786440 | tf_op jit(solution)/shard_map/ppermute | solution.py:20
  125.7 18.6 %collective-permute-start.36 = (bf16[128,1024]{1,0:T(8,128)(2,1)S(1)}, bf16[128,1024]{1,0:T(8,128)(2,1)}, u32[]{:S(2)}, u32[]{:S(2)}) collective-permute-start(bf16[128,1024]{1,0:T(8,128)(2,1)S(1)} %collective-permute-done.35), channel_id=1, source_target_pairs={{0,1},{1,2},{2,3},{3,4},{4,5},{5,6},{6,7},{7,0},{8,9},{9,10},{10,1... | collective-permute-start | bytes 786440 | tf_op jit(solution)/shard_map/ppermute | solution.py:20
  127.2 17.1 %collective-permute-start.41 = (bf16[128,1024]{1,0:T(8,128)(2,1)S(1)}, bf16[128,1024]{1,0:T(8,128)(2,1)}, u32[]{:S(2)}, u32[]{:S(2)}) collective-permute-start(bf16[128,1024]{1,0:T(8,128)(2,1)S(1)} %collective-permute-done.40), channel_id=1, source_target_pairs={{0,7},{1,0},{2,1},{3,2},{4,3},{5,4},{6,5},{7,6},{8,15},{9,8},{10,9... | collective-permute-start | bytes 786440 | tf_op jit(solution)/shard_map/ppermute | solution.py:20
  128.5 18.5 %collective-permute-start.44 = (bf16[128,1024]{1,0:T(8,128)(2,1)}, bf16[128,1024]{1,0:T(8,128)(2,1)}, u32[]{:S(2)}, u32[]{:S(2)}) collective-permute-start(bf16[128,1024]{1,0:T(8,128)(2,1)} %collective-permute-done.43), channel_id=1, source_target_pairs={{0,1},{1,2},{2,3},{3,4},{4,5},{5,6},{6,7},{7,0},{8,9},{9,10},{10,1... | collective-permute-start | bytes 786440 | tf_op jit(solution)/shard_map/ppermute | solution.py:20
  136.7 33.0 %all-to-all-start.1 = ((bf16[4,320,1024]{2,1,0:T(8,128)(2,1)}), bf16[4,320,1024]{2,1,0:T(8,128)(2,1)}, u32[]{:S(2)}, u32[]{:S(2)}) async-start(bf16[4,320,1024]{2,1,0:T(8,128)(2,1)} %bitcast.35), calls=%async_computation.1 | async-start | bytes 5242880 | tf_op jit(solution)/shard_map/all_to_all | solution.py:51
  141.6 23.2 %copy-start.16 = (bf16[128,1024]{1,0:T(8,128)(2,1)S(1)}, bf16[128,1024]{1,0:T(8,128)(2,1)}, u32[]{:S(2)}) copy-start(bf16[128,1024]{1,0:T(8,128)(2,1)} %copy-done.15) | copy-start | bytes 786436
  141.7 10.9 %collective-permute-start.34 = (bf16[128,1024]{1,0:T(8,128)(2,1)}, bf16[128,1024]{1,0:T(8,128)(2,1)S(1)}, u32[]{:S(2)}, u32[]{:S(2)}) collective-permute-start(bf16[128,1024]{1,0:T(8,128)(2,1)} %collective-permute-done.33), channel_id=1, source_target_pairs={{0,7},{1,0},{2,1},{3,2},{4,3},{5,4},{6,5},{7,6},{8,15},{9,8},{10,9... | collective-permute-start | bytes 786440 | tf_op jit(solution)/shard_map/ppermute | solution.py:20
  144.3 8.2 %collective-permute-start.37 = (bf16[128,1024]{1,0:T(8,128)(2,1)}, bf16[128,1024]{1,0:T(8,128)(2,1)S(1)}, u32[]{:S(2)}, u32[]{:S(2)}) collective-permute-start(bf16[128,1024]{1,0:T(8,128)(2,1)} %collective-permute-done.36), channel_id=1, source_target_pairs={{0,1},{1,2},{2,3},{3,4},{4,5},{5,6},{6,7},{7,0},{8,9},{9,10},{10,1... | collective-permute-start | bytes 786440 | tf_op jit(solution)/shard_map/ppermute | solution.py:20
  144.3 13.9 %collective-permute-start.42 = (bf16[128,1024]{1,0:T(8,128)(2,1)}, bf16[128,1024]{1,0:T(8,128)(2,1)S(1)}, u32[]{:S(2)}, u32[]{:S(2)}) collective-permute-start(bf16[128,1024]{1,0:T(8,128)(2,1)} %collective-permute-done.41), channel_id=1, source_target_pairs={{0,7},{1,0},{2,1},{3,2},{4,3},{5,4},{6,5},{7,6},{8,15},{9,8},{10,9... | collective-permute-start | bytes 786440 | tf_op jit(solution)/shard_map/ppermute | solution.py:20
  146.9 11.1 %collective-permute-start.45 = (bf16[128,1024]{1,0:T(8,128)(2,1)}, bf16[128,1024]{1,0:T(8,128)(2,1)S(1)}, u32[]{:S(2)}, u32[]{:S(2)}) collective-permute-start(bf16[128,1024]{1,0:T(8,128)(2,1)} %collective-permute-done.44), channel_id=1, source_target_pairs={{0,1},{1,2},{2,3},{3,4},{4,5},{5,6},{6,7},{7,0},{8,9},{9,10},{10,1... | collective-permute-start | bytes 786440 | tf_op jit(solution)/shard_map/ppermute | solution.py:20
  152.5 9.2 %collective-permute-start.38 = (bf16[128,512]{1,0:T(8,128)(2,1)S(1)}, bf16[128,512]{1,0:T(8,128)(2,1)S(1)}, u32[]{:S(2)}, u32[]{:S(2)}) collective-permute-start(bf16[128,512]{1,0:T(8,128)(2,1)S(1)} %slice.251), channel_id=1, source_target_pairs={{0,1},{1,2},{2,3},{3,4},{4,5},{5,6},{6,7},{7,0},{8,9},{9,10},{10,1... | collective-permute-start | bytes 393224 | tf_op jit(solution)/shard_map/ppermute | solution.py:20
  152.6 9.1 %collective-permute-start.39 = (bf16[128,512]{1,0:T(8,128)(2,1)S(1)}, bf16[128,512]{1,0:T(8,128)(2,1)S(1)}, u32[]{:S(2)}, u32[]{:S(2)}) collective-permute-start(bf16[128,512]{1,0:T(8,128)(2,1)S(1)} %slice.252), channel_id=1, source_target_pairs={{0,7},{1,0},{2,1},{3,2},{4,3},{5,4},{6,5},{7,6},{8,15},{9,8},{10,9... | collective-permute-start | bytes 393224 | tf_op jit(solution)/shard_map/ppermute | solution.py:20
  158.1 17.1 %collective-permute-start.46 = (bf16[128,512]{1,0:T(8,128)(2,1)S(1)}, bf16[128,512]{1,0:T(8,128)(2,1)S(1)}, u32[]{:S(2)}, u32[]{:S(2)}) collective-permute-start(bf16[128,512]{1,0:T(8,128)(2,1)S(1)} %slice.253), channel_id=1, source_target_pairs={{0,1},{1,2},{2,3},{3,4},{4,5},{5,6},{6,7},{7,0},{8,9},{9,10},{10,1... | collective-permute-start | bytes 393224 | tf_op jit(solution)/shard_map/ppermute | solution.py:20
  158.2 17.0 %collective-permute-start.47 = (bf16[128,512]{1,0:T(8,128)(2,1)S(1)}, bf16[128,512]{1,0:T(8,128)(2,1)S(1)}, u32[]{:S(2)}, u32[]{:S(2)}) collective-permute-start(bf16[128,512]{1,0:T(8,128)(2,1)S(1)} %slice.254), channel_id=1, source_target_pairs={{0,7},{1,0},{2,1},{3,2},{4,3},{5,4},{6,5},{7,6},{8,15},{9,8},{10,9... | collective-permute-start | bytes 393224 | tf_op jit(solution)/shard_map/ppermute | solution.py:20
  169.7 25.6 %all-to-all-start.4 = ((bf16[4,320,1024]{2,1,0:T(8,128)(2,1)}), bf16[4,320,1024]{2,1,0:T(8,128)(2,1)}, u32[]{:S(2)}, u32[]{:S(2)}) async-start(bf16[4,320,1024]{2,1,0:T(8,128)(2,1)} %bitcast.78), calls=%async_computation.4 | async-start | bytes 5242880 | tf_op jit(solution)/shard_map/all_to_all | solution.py:51
  195.3 30.9 %all-to-all-start.5 = ((bf16[4,320,1024]{2,1,0:T(8,128)(2,1)}), bf16[4,320,1024]{2,1,0:T(8,128)(2,1)S(1)}, u32[]{:S(2)}, u32[]{:S(2)}) async-start(bf16[4,320,1024]{2,1,0:T(8,128)(2,1)} %bitcast.91), calls=%async_computation.5 | async-start | bytes 5242880 | tf_op jit(solution)/shard_map/all_to_all | solution.py:51
  198.9 166.2 %reduce-scatter.5.cloned.1.call-start = ((), (), s32[]{:S(2)}) async-start(), calls=%async_computation.11 | async-start | bytes 1769472 | tf_op jit(solution)/shard_map/reduce_scatter | solution.py:132
  227.7 30.5 %all-to-all-start.2 = ((bf16[4,320,1024]{2,1,0:T(8,128)(2,1)}), bf16[4,320,1024]{2,1,0:T(8,128)(2,1)S(1)}, u32[]{:S(2)}, u32[]{:S(2)}) async-start(bf16[4,320,1024]{2,1,0:T(8,128)(2,1)} %bitcast.240), calls=%async_computation.2 | async-start | bytes 5242880 | tf_op jit(solution)/shard_map/all_to_all | solution.py:51
  259.7 71.1 %all-to-all-start.3 = ((bf16[4,320,1024]{2,1,0:T(8,128)(2,1)}), bf16[4,320,1024]{2,1,0:T(8,128)(2,1)S(1)}, u32[]{:S(2)}, u32[]{:S(2)}) async-start(bf16[4,320,1024]{2,1,0:T(8,128)(2,1)} %bitcast.238), calls=%async_computation.3 | async-start | bytes 5242880 | tf_op jit(solution)/shard_map/all_to_all | solution.py:51
  263.4 111.5 %reduce-scatter.3.cloned.1.call-start = ((), (), s32[]{:S(2)}) async-start(), calls=%async_computation.10 | async-start | bytes 3538944 | tf_op jit(solution)/shard_map/reduce_scatter | solution.py:133
  327.4 7.4 %collective-permute-start.20 = (bf16[128,512]{1,0:T(8,128)(2,1)}, bf16[128,512]{1,0:T(8,128)(2,1)}, u32[]{:S(2)}, u32[]{:S(2)}) collective-permute-start(bf16[128,512]{1,0:T(8,128)(2,1)} %get-tuple-element.35), channel_id=1, source_target_pairs={{0,7},{1,0},{2,1},{3,2},{4,3},{5,4},{6,5},{7,6},{8,15},{9,8},{10,9... | collective-permute-start | bytes 393224 | tf_op jit(solution)/shard_map/ppermute | solution.py:20
  330.8 7.8 %collective-permute-start.16 = (bf16[128,512]{1,0:T(8,128)(2,1)}, bf16[128,512]{1,0:T(8,128)(2,1)}, u32[]{:S(2)}, u32[]{:S(2)}) collective-permute-start(bf16[128,512]{1,0:T(8,128)(2,1)} %get-tuple-element.34), channel_id=1, source_target_pairs={{0,1},{1,2},{2,3},{3,4},{4,5},{5,6},{6,7},{7,0},{8,9},{9,10},{10,1... | collective-permute-start | bytes 393224 | tf_op jit(solution)/shard_map/ppermute | solution.py:20
  331.8 32.1 %copy-start.3 = (bf16[8,128,1024]{2,1,0:T(8,128)(2,1)}, bf16[8,128,1024]{2,1,0:T(8,128)(2,1)S(1)}, u32[]{:S(2)}) copy-start(bf16[8,128,1024]{2,1,0:T(8,128)(2,1)S(1)} %convolution_convert_fusion.6) | copy-start | bytes 6291460
  331.9 8.1 %collective-permute-start.28 = (bf16[128,512]{1,0:T(8,128)(2,1)S(1)}, bf16[128,512]{1,0:T(8,128)(2,1)S(1)}, u32[]{:S(2)}, u32[]{:S(2)}) collective-permute-start(bf16[128,512]{1,0:T(8,128)(2,1)S(1)} %get-tuple-element.37), channel_id=1, source_target_pairs={{0,7},{1,0},{2,1},{3,2},{4,3},{5,4},{6,5},{7,6},{8,15},{9,8},{10,9... | collective-permute-start | bytes 393224 | tf_op jit(solution)/shard_map/ppermute | solution.py:20
  334.7 5.2 %collective-permute-start.24 = (bf16[128,512]{1,0:T(8,128)(2,1)S(1)}, bf16[128,512]{1,0:T(8,128)(2,1)S(1)}, u32[]{:S(2)}, u32[]{:S(2)}) collective-permute-start(bf16[128,512]{1,0:T(8,128)(2,1)S(1)} %get-tuple-element.36), channel_id=1, source_target_pairs={{0,1},{1,2},{2,3},{3,4},{4,5},{5,6},{6,7},{7,0},{8,9},{9,10},{10,1... | collective-permute-start | bytes 393224 | tf_op jit(solution)/shard_map/ppermute | solution.py:20
  335.9 13.6 %collective-permute-start.21 = (bf16[128,1024]{1,0:T(8,128)(2,1)S(1)}, bf16[128,1024]{1,0:T(8,128)(2,1)S(1)}, u32[]{:S(2)}, u32[]{:S(2)}) collective-permute-start(bf16[128,1024]{1,0:T(8,128)(2,1)S(1)} %pad_maximum_fusion.5), channel_id=1, source_target_pairs={{0,7},{1,0},{2,1},{3,2},{4,3},{5,4},{6,5},{7,6},{8,15},{9,8},{10,9... | collective-permute-start | bytes 786440 | tf_op jit(solution)/shard_map/ppermute | solution.py:20
  339.5 6.7 %collective-permute-start.17 = (bf16[128,1024]{1,0:T(8,128)(2,1)S(1)}, bf16[128,1024]{1,0:T(8,128)(2,1)S(1)}, u32[]{:S(2)}, u32[]{:S(2)}) collective-permute-start(bf16[128,1024]{1,0:T(8,128)(2,1)S(1)} %pad_maximum_fusion.4), channel_id=1, source_target_pairs={{0,1},{1,2},{2,3},{3,4},{4,5},{5,6},{6,7},{7,0},{8,9},{9,10},{10,1... | collective-permute-start | bytes 786440 | tf_op jit(solution)/shard_map/ppermute | solution.py:20
  340.0 9.2 %collective-permute-start.25 = (bf16[128,1024]{1,0:T(8,128)(2,1)S(1)}, bf16[128,1024]{1,0:T(8,128)(2,1)S(1)}, u32[]{:S(2)}, u32[]{:S(2)}) collective-permute-start(bf16[128,1024]{1,0:T(8,128)(2,1)S(1)} %pad_maximum_fusion.6), channel_id=1, source_target_pairs={{0,1},{1,2},{2,3},{3,4},{4,5},{5,6},{6,7},{7,0},{8,9},{9,10},{10,1... | collective-permute-start | bytes 786440 | tf_op jit(solution)/shard_map/ppermute | solution.py:20
  340.1 13.3 %collective-permute-start.29 = (bf16[128,1024]{1,0:T(8,128)(2,1)S(1)}, bf16[128,1024]{1,0:T(8,128)(2,1)S(1)}, u32[]{:S(2)}, u32[]{:S(2)}) collective-permute-start(bf16[128,1024]{1,0:T(8,128)(2,1)S(1)} %pad_maximum_fusion.7), channel_id=1, source_target_pairs={{0,7},{1,0},{2,1},{3,2},{4,3},{5,4},{6,5},{7,6},{8,15},{9,8},{10,9... | collective-permute-start | bytes 786440 | tf_op jit(solution)/shard_map/ppermute | solution.py:20
  346.3 6.9 %collective-permute-start.18 = (bf16[128,1024]{1,0:T(8,128)(2,1)S(1)}, bf16[128,1024]{1,0:T(8,128)(2,1)S(1)}, u32[]{:S(2)}, u32[]{:S(2)}) collective-permute-start(bf16[128,1024]{1,0:T(8,128)(2,1)S(1)} %fusion.24), channel_id=1, source_target_pairs={{0,1},{1,2},{2,3},{3,4},{4,5},{5,6},{6,7},{7,0},{8,9},{9,10},{10,1... | collective-permute-start | bytes 786440 | tf_op jit(solution)/shard_map/ppermute | solution.py:20
  349.2 6.8 %collective-permute-start.26 = (bf16[128,1024]{1,0:T(8,128)(2,1)S(1)}, bf16[128,1024]{1,0:T(8,128)(2,1)S(1)}, u32[]{:S(2)}, u32[]{:S(2)}) collective-permute-start(bf16[128,1024]{1,0:T(8,128)(2,1)S(1)} %fusion.18), channel_id=1, source_target_pairs={{0,1},{1,2},{2,3},{3,4},{4,5},{5,6},{6,7},{7,0},{8,9},{9,10},{10,1... | collective-permute-start | bytes 786440 | tf_op jit(solution)/shard_map/ppermute | solution.py:20
  353.4 5.6 %collective-permute-start.22 = (bf16[128,1024]{1,0:T(8,128)(2,1)S(1)}, bf16[128,1024]{1,0:T(8,128)(2,1)S(1)}, u32[]{:S(2)}, u32[]{:S(2)}) collective-permute-start(bf16[128,1024]{1,0:T(8,128)(2,1)S(1)} %get-tuple-element.15), channel_id=1, source_target_pairs={{0,7},{1,0},{2,1},{3,2},{4,3},{5,4},{6,5},{7,6},{8,15},{9,8},{10,9... | collective-permute-start | bytes 786440 | tf_op jit(solution)/shard_map/ppermute | solution.py:20
  356.9 7.0 %collective-permute-start.30 = (bf16[128,1024]{1,0:T(8,128)(2,1)S(1)}, bf16[128,1024]{1,0:T(8,128)(2,1)S(1)}, u32[]{:S(2)}, u32[]{:S(2)}) collective-permute-start(bf16[128,1024]{1,0:T(8,128)(2,1)S(1)} %get-tuple-element.20), channel_id=1, source_target_pairs={{0,7},{1,0},{2,1},{3,2},{4,3},{5,4},{6,5},{7,6},{8,15},{9,8},{10,9... | collective-permute-start | bytes 786440 | tf_op jit(solution)/shard_map/ppermute | solution.py:20
  357.5 10.0 %collective-permute-start.19 = (bf16[128,1024]{1,0:T(8,128)(2,1)S(1)}, bf16[128,1024]{1,0:T(8,128)(2,1)}, u32[]{:S(2)}, u32[]{:S(2)}) collective-permute-start(bf16[128,1024]{1,0:T(8,128)(2,1)S(1)} %get-tuple-element.14), channel_id=1, source_target_pairs={{0,1},{1,2},{2,3},{3,4},{4,5},{5,6},{6,7},{7,0},{8,9},{9,10},{10,1... | collective-permute-start | bytes 786440 | tf_op jit(solution)/shard_map/ppermute | solution.py:20
  359.0 10.4 %collective-permute-start.27 = (bf16[128,1024]{1,0:T(8,128)(2,1)}, bf16[128,1024]{1,0:T(8,128)(2,1)}, u32[]{:S(2)}, u32[]{:S(2)}) collective-permute-start(bf16[128,1024]{1,0:T(8,128)(2,1)} %get-tuple-element.19), channel_id=1, source_target_pairs={{0,1},{1,2},{2,3},{3,4},{4,5},{5,6},{6,7},{7,0},{8,9},{9,10},{10,1... | collective-permute-start | bytes 786440 | tf_op jit(solution)/shard_map/ppermute | solution.py:20
  359.1 9.1 %collective-permute-start.23 = (bf16[128,1024]{1,0:T(8,128)(2,1)S(1)}, bf16[128,1024]{1,0:T(8,128)(2,1)}, u32[]{:S(2)}, u32[]{:S(2)}) collective-permute-start(bf16[128,1024]{1,0:T(8,128)(2,1)S(1)} %fusion.23), channel_id=1, source_target_pairs={{0,7},{1,0},{2,1},{3,2},{4,3},{5,4},{6,5},{7,6},{8,15},{9,8},{10,9... | collective-permute-start | bytes 786440 | tf_op jit(solution)/shard_map/ppermute | solution.py:20
  364.0 9.7 %collective-permute-start.31 = (bf16[128,1024]{1,0:T(8,128)(2,1)S(1)}, bf16[128,1024]{1,0:T(8,128)(2,1)}, u32[]{:S(2)}, u32[]{:S(2)}) collective-permute-start(bf16[128,1024]{1,0:T(8,128)(2,1)S(1)} %fusion.17), channel_id=1, source_target_pairs={{0,7},{1,0},{2,1},{3,2},{4,3},{5,4},{6,5},{7,6},{8,15},{9,8},{10,9... | collective-permute-start | bytes 786440 | tf_op jit(solution)/shard_map/ppermute | solution.py:20
  (18 other events, 76.5 us)
Sparse Core Ops, SparseCore 0:
  9.9 31.9 all-gather.4
  43.7 31.3 all-gather.6
  204.4 57.4 reduce-scatter.4
  270.3 63.1 reduce-scatter.2
